TPU v7x, 512 devices: a whole 4x4x16 slice. The times are simulated.
512 devices in a mesh: batch: 16 (over z_hi, y, core), tensor: 32 (over x, z_lo).
Axes of the slice: x: 4, y: 4, z: 16 (z_hi: 2, z_lo: 8; z = z_hi * 8 + z_lo), core: 2. Of those that a mesh axis runs over, the one named last changes fastest.
Arguments:
- tokens: bfloat16 [4096, 4096], P('batch', 'tensor'), may hold values from -6 to 6
- gate_pre: bfloat16 [4096, 14336], P('batch', 'tensor'), may hold values from -8 to 8
- up_pre: bfloat16 [4096, 14336], P('batch', 'tensor'), may hold values from -6 to 6
- down_weight: bfloat16 [14336, 4096], P('tensor'), may hold values from -0.046875 to 0.046875
- tangent_gate: bfloat16 [4096, 14336], P('batch', 'tensor'), may hold values from -0.09375 to 0.09375
- loss_weight: float32 [4096], P('batch'), may hold values from 0.05 to 0.5
Outputs:
- gnvp: float32 [4096, 14336], P('batch', 'tensor')
All inputs are finite; a program needn't handle non-finite values.
Results may differ from a plain program's by a relative error of at most 0.025.
Values may be sent and summed in bfloat16 or wider, within the bound.
A program may use at most 64 MiB of HBM per device.

v0:
```python
import jax
import jax.numpy as jnp
from jax import lax
from jax.sharding import PartitionSpec as P


def slope_of(gate_pre, up_pre):
    a = gate_pre.astype(jnp.float32)
    sig = jax.nn.sigmoid(a)
    return sig * (1.0 + a * (1.0 - sig)) * up_pre.astype(jnp.float32)


def body(tokens, gate_pre, up_pre, down_weight, tangent_gate, loss_weight):
    whole = lax.all_gather(tokens, "tensor", axis=1, tiled=True)
    slope = slope_of(gate_pre, up_pre)
    columns = whole
    tangent_gate_out = jnp.dot(
        columns,
        lax.all_gather(tangent_gate, "batch", axis=0, tiled=True),
        preferred_element_type=jnp.float32,
    )
    tangent_hidden = (slope * tangent_gate_out).astype(jnp.bfloat16)
    partial_out = jnp.dot(tangent_hidden, down_weight, preferred_element_type=jnp.float32)
    tangent_out = lax.psum(partial_out.astype(jnp.bfloat16), "tensor").astype(jnp.float32)
    weighted = (loss_weight[:, None] * tangent_out).astype(jnp.bfloat16)
    back_hidden = jnp.einsum("td,fd->tf", weighted, down_weight, preferred_element_type=jnp.float32)
    back_gate = (back_hidden * slope).astype(jnp.bfloat16)
    columns = whole
    return lax.psum_scatter(
        jnp.einsum("td,tf->df", columns, back_gate, preferred_element_type=jnp.float32).astype(
            jnp.bfloat16
        ),
        "batch",
        scatter_dimension=0,
        tiled=True,
    ).astype(jnp.float32)


def solution(mesh):
    placed = (
        P("batch", "tensor"),
        P("batch", "tensor"),
        P("batch", "tensor"),
        P("tensor", None),
        P("batch", "tensor"),
        P("batch"),
    )
    return jax.shard_map(
        body, mesh=mesh, in_specs=placed, out_specs=P("batch", "tensor"), check_vma=False
    )
```

profile of v0, /device:TPU:2, one launch (start us, length us, event | category | flops | bytes accessed | tf_op | source)
XLA Modules:
  0.0 940.3 jit_solution(17871154214957523726)
XLA Ops:
  6.5 0.0 all-gather.3.cloned.1.call-start
  6.5 0.7 all-gather.3.cloned.1.call-update
  7.3 0.0 all-gather.5.cloned.1.call-start
  7.3 0.7 all-gather.5.cloned.1.call-update
  8.0 0.0 copy-start.1
  8.0 0.0 copy-start.2
  8.0 0.0 copy-start.3
  8.0 0.0 all-reduce.2.cloned.1.call-start
  8.1 183.1 %all-gather.3.cloned.1.call-done = bf16[256,4096]{1,0:T(8,128)(2,1)} async-done(((bf16[256,128]{1,0:T(8,128)(2,1)}), bf16[256,4096]{1,0:T(8,128)(2,1)}) %all-gather.3.cloned.1.call-update) | async-done | bytes 2097168 | tf_op jit(solution)/shard_map/all_gather | solution.py:14
  191.1 0.0 copy-start
  191.1 120.4 %all-gather.5.cloned.1.call-done = bf16[4096,448]{0,1:T(8,128)(2,1)} async-done(((bf16[256,448]{0,1:T(8,128)(2,1)}), bf16[4096,448]{0,1:T(8,128)(2,1)}) %all-gather.5.cloned.1.call-update) | async-done | bytes 3670032 | tf_op jit(solution)/shard_map/all_gather | solution.py:19
  311.5 9.6 %convolution_convert_fusion.1 = bf16[256,4096]{1,0:T(8,128)(2,1)} fusion(bf16[448,4096]{1,0:T(8,128)(2,1)} %param.9, bf16[256,4096]{1,0:T(8,128)(2,1)} %all-gather.3.cloned.1.call-done, bf16[4096,448]{0,1:T(8,128)(2,1)} %all-gather.5.cloned.1.call-done, bf16[256,448]{0,1:T(8,128)(2,1)} %param.7, bf16[256,448]{0,1:T(8,128)(2,1)} %param.8), kind=kOutput, calls=%fused_computation.2 | convolution fusion | flops 1881473024 | bytes 11993088 | tf_op jit(solution)/shard_map/dot_general | solution.py:23
  321.1 0.0 all-reduce.2.cloned.1.call-update
  321.1 0.0 reduce-scatter.2.cloned.1.call-start
  321.2 440.5 %all-reduce.2.cloned.1.call-done = bf16[256,4096]{1,0:T(8,128)(2,1)} async-done(((bf16[256,4096]{1,0:T(8,128)(2,1)}), bf16[256,4096]{1,0:T(8,128)(2,1)}) %all-reduce.2.cloned.1.call-update) | async-done | bytes 2097168 | tf_op jit(solution)/shard_map/psum | solution.py:24
  761.7 0.0 copy-done.1
  761.7 0.0 copy-done.2
  761.7 0.0 copy-done.3
  761.7 0.0 copy-done
  761.7 8.6 fusion
  770.3 0.0 reduce-scatter.2.cloned.1.call-update
  770.3 161.8 %reduce-scatter.2.cloned.1.call-done = bf16[256,448]{0,1:T(8,128)(2,1)} async-done(((bf16[4096,448]{0,1:T(8,128)(2,1)}), bf16[256,448]{0,1:T(8,128)(2,1)}) %reduce-scatter.2.cloned.1.call-update) | async-done | bytes 229392 | tf_op jit(solution)/shard_map/reduce_scatter | solution.py:29
  932.1 1.7 convert_element_type.39
Async XLA Ops:
  6.5 184.6 %all-gather.3.cloned.1.call-start = ((), (), s32[]{:S(2)}) async-start(), calls=%async_computation.1 | async-start | bytes 2162688 | tf_op jit(solution)/shard_map/all_gather | solution.py:14
  7.3 304.3 %all-gather.5.cloned.1.call-start = ((), (), s32[]{:S(2)}) async-start(), calls=%async_computation.2 | async-start | bytes 3899392 | tf_op jit(solution)/shard_map/all_gather | solution.py:19
  8.0 753.7 %copy-start.1 = (bf16[256,448]{0,1:T(8,128)(2,1)S(1)}, bf16[256,448]{0,1:T(8,128)(2,1)}, u32[]{:S(2)}) copy-start(bf16[256,448]{0,1:T(8,128)(2,1)} %param.7) | copy-start | bytes 688132
  8.0 753.7 %copy-start.2 = (bf16[256,448]{0,1:T(8,128)(2,1)S(1)}, bf16[256,448]{0,1:T(8,128)(2,1)}, u32[]{:S(2)}) copy-start(bf16[256,448]{0,1:T(8,128)(2,1)} %param.8) | copy-start | bytes 688132
  8.0 753.7 %copy-start.3 = (f32[256]{0:T(256)S(1)}, f32[256]{0:T(256)}, u32[]{:S(2)}) copy-start(f32[256]{0:T(256)} %param.11) | copy-start | bytes 3076
  8.0 753.6 %all-reduce.2.cloned.1.call-start = ((), (), s32[]{:S(2)}) async-start(), calls=%async_computation.3 | async-start | bytes 4194304 | tf_op jit(solution)/shard_map/psum | solution.py:24
  191.1 570.5 %copy-start = (bf16[256,4096]{1,0:T(8,128)(2,1)S(1)}, bf16[256,4096]{1,0:T(8,128)(2,1)}, u32[]{:S(2)}) copy-start(bf16[256,4096]{1,0:T(8,128)(2,1)} %all-gather.3.cloned.1.call-done) | copy-start | bytes 6291460
  321.1 610.9 %reduce-scatter.2.cloned.1.call-start = ((), (), s32[]{:S(2)}) async-start(), calls=%async_computation.4 | async-start | bytes 3899392 | tf_op jit(solution)/shard_map/reduce_scatter | solution.py:29
Sparse Core Ops, SparseCore 0:
  9.4 181.7 all-gather.2
  194.3 117.2 all-gather.4
  321.2 440.3 all-reduce.1
  770.4 161.6 reduce-scatter.1
where the time goes:
time: 940 us
  waiting for transfers between devices  907 us (96%)
  matrix products  18.1 us (2%)
  between operations  13.2 us (1%)
    psum x1, waiting for transfers between devices, body(): lax.psum(partial_out.astype(jnp.bfloat16), 'tensor').astype(jnp.float32)  441 us
    all_gather x1, waiting for transfers between devices, body(): whole = lax.all_gather(tokens, 'tensor', axis=1, tiled=True)  183 us
    reduce_scatter x1, waiting for transfers between devices, body(): lax.psum_scatter(jnp.einsum('td,tf->df', columns, back_gate, preferred_el...  162 us
    all_gather x1, waiting for transfers between devices, body(): lax.all_gather(tangent_gate, 'batch', axis=0, tiled=True)  120 us
  transfers between devices with their start and end apart: 4, of which 4 were waited for; matrix products, arithmetic and copies ran while one was open for 0% of the time, Pallas kernels for 0%

commit v1 on v0

--- a/solution.py
+++ b/solution.py
@@ -16,7 +16,10 @@
     columns = whole
     tangent_gate_out = jnp.dot(
         columns,
-        lax.all_gather(tangent_gate, "batch", axis=0, tiled=True),
+        jnp.concatenate(
+            lax.all_to_all(jnp.stack([tangent_gate] * lax.axis_size("batch")), "batch", 0, 0),
+            axis=0,
+        ),
         preferred_element_type=jnp.float32,
     )
     tangent_hidden = (slope * tangent_gate_out).astype(jnp.bfloat16)

time: 940 us -> 971 us (1.033)
  starting transfers between devices: 0.12 us -> 18 us
    all_gather x1 -> x0, waiting for transfers between devices: 120 us -> none  [body(): lax.all_gather(tangent_gate, 'batch', axis=0, tiled=True)]
    all_to_all x0 -> x1, waiting for transfers between devices: none -> 97.6 us  [body(): lax.all_to_all(jnp.stack([tangent_gate] * lax.axis_size('batch')), 'batch...]
    all_gather x1, waiting for transfers between devices: 183 us -> 202 us  [body(): whole = lax.all_gather(tokens, 'tensor', axis=1, tiled=True)]
    all_to_all x0 -> x1, starting transfers between devices: none -> 17.9 us  [body(): lax.all_to_all(jnp.stack([tangent_gate] * lax.axis_size('batch')), 'batch...]
    psum x1, waiting for transfers between devices: 441 us -> 451 us  [body(): lax.psum(partial_out.astype(jnp.bfloat16), 'tensor').astype(jnp.float32)]
where the time goes in v1:
time: 971 us
  waiting for transfers between devices  912 us (94%)
  matrix products  18.1 us (2%)
  starting transfers between devices  18 us (2%)
  between operations  13.1 us (1%)
    psum x1, waiting for transfers between devices, body(): lax.psum(partial_out.astype(jnp.bfloat16), 'tensor').astype(jnp.float32)  451 us
    all_gather x1, waiting for transfers between devices, body(): whole = lax.all_gather(tokens, 'tensor', axis=1, tiled=True)  202 us
    reduce_scatter x1, waiting for transfers between devices, body(): lax.psum_scatter(jnp.einsum('td,tf->df', columns, back_gate, preferred_el...  162 us
    all_to_all x1, waiting for transfers between devices, body(): lax.all_to_all(jnp.stack([tangent_gate] * lax.axis_size('batch')), 'batch...  97.6 us
  transfers between devices with their start and end apart: 4, of which 4 were waited for; matrix products, arithmetic and copies ran while one was open for 0% of the time, Pallas kernels for 0%

profile of v1, /device:TPU:2, one launch (start us, length us, event | category | flops | bytes accessed | tf_op | source)
XLA Modules:
  0.0 970.8 jit_solution(17477427549754074123)
XLA Ops:
  6.5 3.1 stack.2
  9.6 17.9 %all-to-all-start = ((bf16[16,256,448]{1,2,0:T(8,128)(2,1)}), bf16[16,256,448]{1,2,0:T(8,128)(2,1)}, u32[]{:S(2)}, u32[]{:S(2)}) async-start(bf16[16,256,448]{1,2,0:T(8,128)(2,1)} %stack.2), calls=%async_computation | async-start | bytes 7340032 | tf_op jit(solution)/shard_map/all_to_all | solution.py:20
  27.5 0.0 all-gather.2.cloned.1.call-start
  27.6 0.7 all-gather.2.cloned.1.call-update
  28.3 0.0 all-reduce.2.cloned.1.call-start
  28.3 97.6 %all-to-all-done = bf16[16,256,448]{1,2,0:T(8,128)(2,1)} async-done(((bf16[16,256,448]{1,2,0:T(8,128)(2,1)}), bf16[16,256,448]{1,2,0:T(8,128)(2,1)}, u32[]{:S(2)}, u32[]{:S(2)}) %all-to-all-start) | async-done | bytes 3670048 | tf_op jit(solution)/shard_map/all_to_all | solution.py:20
  125.9 0.0 copy-start.1
  125.9 0.0 copy-start.2
  125.9 4.4 copy.9
  130.3 201.7 %all-gather.2.cloned.1.call-done = bf16[256,4096]{1,0:T(8,128)(2,1)} async-done(((bf16[256,128]{1,0:T(8,128)(2,1)}), bf16[256,4096]{1,0:T(8,128)(2,1)}) %all-gather.2.cloned.1.call-update) | async-done | bytes 2097168 | tf_op jit(solution)/shard_map/all_gather | solution.py:14
  332.0 0.0 copy-done.1
  332.1 0.0 copy-done.2
  332.1 0.0 copy-start
  332.1 0.0 copy-start.3
  332.1 9.5 convolution_convert_fusion.1
  341.6 0.0 all-reduce.2.cloned.1.call-update
  341.6 0.0 reduce-scatter.2.cloned.1.call-start
  341.7 450.5 %all-reduce.2.cloned.1.call-done = bf16[256,4096]{1,0:T(8,128)(2,1)} async-done(((bf16[256,4096]{1,0:T(8,128)(2,1)}), bf16[256,4096]{1,0:T(8,128)(2,1)}) %all-reduce.2.cloned.1.call-update) | async-done | bytes 2097168 | tf_op jit(solution)/shard_map/psum | solution.py:27
  792.2 0.0 copy-done
  792.2 0.0 copy-done.3
  792.2 8.6 fusion
  800.7 0.0 reduce-scatter.2.cloned.1.call-update
  800.8 161.8 %reduce-scatter.2.cloned.1.call-done = bf16[256,448]{0,1:T(8,128)(2,1)} async-done(((bf16[4096,448]{0,1:T(8,128)(2,1)}), bf16[256,448]{0,1:T(8,128)(2,1)}) %reduce-scatter.2.cloned.1.call-update) | async-done | bytes 229392 | tf_op jit(solution)/shard_map/reduce_scatter | solution.py:32
  962.5 1.7 convert_element_type.39
Async XLA Ops:
  9.6 116.2 %all-to-all-start = ((bf16[16,256,448]{1,2,0:T(8,128)(2,1)}), bf16[16,256,448]{1,2,0:T(8,128)(2,1)}, u32[]{:S(2)}, u32[]{:S(2)}) async-start(bf16[16,256,448]{1,2,0:T(8,128)(2,1)} %stack.2), calls=%async_computation | async-start | bytes 7340032 | tf_op jit(solution)/shard_map/all_to_all | solution.py:20
  27.5 304.5 %all-gather.2.cloned.1.call-start = ((), (), s32[]{:S(2)}) async-start(), calls=%async_computation.2 | async-start | bytes 2162688 | tf_op jit(solution)/shard_map/all_gather | solution.py:14
  28.3 763.9 %all-reduce.2.cloned.1.call-start = ((), (), s32[]{:S(2)}) async-start(), calls=%async_computation.3 | async-start | bytes 4194304 | tf_op jit(solution)/shard_map/psum | solution.py:27
  125.9 206.2 %copy-start.1 = (bf16[256,448]{0,1:T(8,128)(2,1)S(1)}, bf16[256,448]{0,1:T(8,128)(2,1)}, u32[]{:S(2)}) copy-start(bf16[256,448]{0,1:T(8,128)(2,1)} %param.7) | copy-start | bytes 688132
  125.9 206.2 %copy-start.2 = (bf16[256,448]{0,1:T(8,128)(2,1)S(1)}, bf16[256,448]{0,1:T(8,128)(2,1)}, u32[]{:S(2)}) copy-start(bf16[256,448]{0,1:T(8,128)(2,1)} %param.8) | copy-start | bytes 688132
  332.1 460.1 %copy-start = (bf16[256,4096]{1,0:T(8,128)(2,1)S(1)}, bf16[256,4096]{1,0:T(8,128)(2,1)}, u32[]{:S(2)}) copy-start(bf16[256,4096]{1,0:T(8,128)(2,1)} %all-gather.2.cloned.1.call-done) | copy-start | bytes 6291460
  332.1 460.1 %copy-start.3 = (f32[256]{0:T(256)S(1)}, f32[256]{0:T(256)}, u32[]{:S(2)}) copy-start(f32[256]{0:T(256)} %param.11) | copy-start | bytes 3076
  341.6 620.9 %reduce-scatter.2.cloned.1.call-start = ((), (), s32[]{:S(2)}) async-start(), calls=%async_computation.4 | async-start | bytes 3899392 | tf_op jit(solution)/shard_map/reduce_scatter | solution.py:32
Sparse Core Ops, SparseCore 0:
  30.4 301.6 all-gather.1
  341.7 450.4 all-reduce.1
  800.9 161.5 reduce-scatter.1
